TPU v7x, 32 devices: a whole 2x2x4 slice. The times are simulated.
32 devices in a mesh: case: 2 (over x), leaf: 16 (over z, y, core).
Axes of the slice: x: 2, y: 2, z: 4, core: 2. Of those that a mesh axis runs over, the one named last changes fastest.
Arguments:
- fields: bfloat16 [512, 2, 128, 128], P(('case', 'leaf')), parts along dimension 0, may hold values from -6 to 6
- own_factor: bfloat16 [4, 512, 2, 128, 128], P(None, ('case', 'leaf')), parts along dimension 1, may hold values from -0.25 to 0.25
- partner_factor: bfloat16 [4, 512, 2, 128, 128], P(None, ('case', 'leaf')), parts along dimension 1, may hold values from -0.25 to 0.25
- near_blocks: bfloat16 [1024, 2, 128, 128], P(('case', 'leaf')), parts along dimension 0, may hold values from -0.375 to 0.375
- near_pairs: int32 [512, 2], P('leaf'), may hold values from 0 to 31, as said below
- near_count: int32 [16], P('leaf'), may hold values from 16 to 32, as said below
Outputs:
- scattered: bfloat16 [512, 2, 128, 128], P(('case', 'leaf')), parts along dimension 0
There are 2 independent parts, one for each index of `case`. A program takes and returns all parts, laid end to end along the dimension named above; an argument that names none is the same for every part. Nothing has to cross between parts.
Inputs may be any that keep to these rules, and one draw needn't show every extreme that they name: `near_pairs`: column 0 is a box position 0 to 15. Column 1 always names an existing box: on the first device it is at least 8, on the last at most 23. `near_count`: some device has all 32 slots live.
All inputs are finite; a program needn't handle non-finite values.
Results may differ from a plain program's by a relative error of at most 0.0055.
Values may be sent and summed in bfloat16 or wider, within the bound.
A program may use at most 64 MiB of HBM per device.

v0:
```python
import jax
import jax.numpy as jnp
from jax import lax
from jax.sharding import PartitionSpec as P


def with_halo(shard, sides, width):
    for axis, dim in sides:
        devices, length = (lax.axis_size(axis), shard.shape[dim])
        up = [(i, (i + 1) % devices) for i in range(devices - 1)]
        down = [(j, i) for i, j in up]
        last = lax.slice_in_dim(shard, length - width, length, axis=dim)
        first = lax.slice_in_dim(shard, 0, width, axis=dim)
        before = lax.ppermute(last, axis, up)
        after = lax.ppermute(first, axis, down)
        shard = jnp.concatenate([before, shard, after], axis=dim)
    return shard


def swapped(value, axis, apart):
    mask = 2**apart
    pairs = [(source, source ^ mask) for source in range(lax.axis_size(axis))]
    return lax.ppermute(value, axis, pairs)


def complex_apply(weight, vec):
    wr = weight[:, 0]
    wi = weight[:, 1]
    vr = vec[:, 0]
    vi = vec[:, 1]
    form = "nij,njr->nir"
    real = jnp.einsum(form, wr, vr, preferred_element_type=jnp.float32) - jnp.einsum(
        form, wi, vi, preferred_element_type=jnp.float32
    )
    imag = jnp.einsum(form, wr, vi, preferred_element_type=jnp.float32) + jnp.einsum(
        form, wi, vr, preferred_element_type=jnp.float32
    )
    return jnp.stack([real, imag], axis=1)


def per_device(fields, own_factor, partner_factor, near_blocks, near_pairs, near_count):
    box_count = fields.shape[0]
    slot_count = near_blocks.shape[0]
    reach = box_count // 2
    depth = lax.axis_size("leaf").bit_length() - 1
    levels = own_factor.shape[0]
    widened = with_halo(fields, (("leaf", 0),), reach)
    sources = jnp.take(widened, near_pairs[:, 1], axis=0)
    products = complex_apply(near_blocks, sources)
    live = jnp.arange(slot_count, dtype=jnp.int32) < near_count[0]
    picks = (near_pairs[:, 0][None, :] == jnp.arange(box_count, dtype=jnp.int32)[:, None]) & live[
        None, :
    ]
    near = jnp.dot(
        picks.astype(jnp.float32), products.reshape(slot_count, -1), precision=lax.Precision.HIGHEST
    )
    near = near.reshape(fields.shape)
    section = fields
    for level in range(levels):
        bit = depth - 1 - level
        partner = swapped(section, "leaf", bit)
        total = complex_apply(own_factor[level], section) + complex_apply(
            partner_factor[level], partner
        )
        section = total.astype(jnp.bfloat16)
    return (section.astype(jnp.float32) + near).astype(jnp.bfloat16)


def solution(mesh):
    in_specs = (
        P(("case", "leaf"), None, None, None),
        P(None, ("case", "leaf"), None, None, None),
        P(None, ("case", "leaf"), None, None, None),
        P(("case", "leaf"), None, None, None),
        P("leaf", None),
        P("leaf"),
    )
    out_specs = P(("case", "leaf"), None, None, None)
    return jax.shard_map(
        per_device, mesh=mesh, in_specs=in_specs, out_specs=out_specs, check_vma=False
    )
```

profile of v0, /device:TPU:0, one launch (start us, length us, event | category | flops | bytes accessed | tf_op | source)
XLA Modules:
  0.0 136.8 jit_solution(6378273048907898273)
XLA Ops:
  0.0 2.5 %copy.31 = bf16[16,2,128,128]{3,2,0,1:T(8,128)(2,1)} copy(bf16[16,2,128,128]{3,2,1,0:T(8,128)(2,1)} %param.6) | data formatting | bytes 2097152 | tf_op args[0]
  2.5 4.0 %collective-permute-start = (bf16[16,2,128,128]{3,2,0,1:T(8,128)(2,1)}, bf16[16,2,128,128]{3,2,0,1:T(8,128)(2,1)}, u32[]{:S(2)}, u32[]{:S(2)}) collective-permute-start(bf16[16,2,128,128]{3,2,0,1:T(8,128)(2,1)} %copy.31), channel_id=1, source_target_pairs={{0,8},{1,9},{2,10},{3,11},{4,12},{5,13},{6,14},{7,15},{8,0},{9,1},... | collective-permute-start | bytes 3145736 | tf_op jit(solution)/shard_map/ppermute | solution.py:23
  6.6 1.5 %collective-permute-start.4 = (bf16[8,2,128,128]{3,2,1,0:T(8,128)(2,1)S(1)}, bf16[8,2,128,128]{3,2,1,0:T(8,128)(2,1)S(1)}, u32[]{:S(2)}, u32[]{:S(2)}) collective-permute-start(bf16[8,2,128,128]{3,2,1,0:T(8,128)(2,1)S(1)} %get-tuple-element.13), channel_id=1, source_target_pairs={{0,1},{1,2},{2,3},{3,4},{4,5},{5,6},{6,7},{7,8},{8,9},{9,10},{10,1... | collective-permute-start | bytes 1572872 | tf_op jit(solution)/shard_map/ppermute | solution.py:14
  8.1 1.3 collective-permute-start.5
  9.4 2.8 %fusion.54 = (bf16[1,16,2,128,128]{4,3,2,1,0:T(8,128)(2,1)S(1)}, bf16[1,16,2,128,128]{4,3,2,1,0:T(8,128)(2,1)S(1)}, bf16[1,16,2,128,128]{4,3,2,1,0:T(8,128)(2,1)S(1)}, bf16[1,16,2,128,128]{4,3,2,1,0:T(8,128)(2,1)S(1)}) fusion(bf16[4,16,2,128,128]{4,3,2,1,0:T(8,128)(2,1)} %param.7), kind=kLoop, calls=%fused_computation.129 | loop fusion | bytes 8388608 | tf_op jit(solution)/shard_map/slice | solution.py:62
  12.9 1.6 %copy-done.9 = bf16[4,16,2,128,128]{4,3,2,1,0:T(8,128)(2,1)S(1)} copy-done((bf16[4,16,2,128,128]{4,3,2,1,0:T(8,128)(2,1)S(1)}, bf16[4,16,2,128,128]{4,3,2,1,0:T(8,128)(2,1)}, u32[]{:S(2)}) %copy-start.9) | copy-done | bytes 4194328
  14.5 0.6 fusion.55
  15.1 1.1 copy.107
  16.2 1.3 fusion.20
  17.5 1.1 copy.106
  18.6 1.2 copy.103
  19.8 1.1 copy.104
  22.3 1.3 fusion.21
  23.6 1.6 %pad_maximum_fusion.1 = bf16[32,2,128,128]{3,2,1,0:T(8,128)(2,1)} fusion(bf16[8,2,128,128]{3,2,1,0:T(8,128)(2,1)S(1)} %collective-permute-done.5, bf16[16,2,128,128]{3,2,1,0:T(8,128)(2,1)S(1)} %copy-done, bf16[8,2,128,128]{3,2,1,0:T(8,128)(2,1)S(1)} %collective-permute-done.4), kind=kLoop, calls=%fused_computation.13 | loop fusion | flops 2097152 | bytes 4194304 | tf_op jit(solution)/shard_map/concatenate | solution.py:16
  25.1 3.7 %gather_fusion = bf16[32,2,128,128]{3,2,1,0:T(8,128)(2,1)} fusion(bf16[32,2,128,128]{3,2,1,0:T(8,128)(2,1)} %pad_maximum_fusion.1, s32[1024]{0:T(1024)S(1)} %pad_clamp_fusion), kind=kCustom, calls=%fused_computation | custom fusion | bytes 4194432 | tf_op jit(solution)/shard_map/jit(_take)/gather | solution.py:48
  28.8 4.1 %copy.49 = bf16[32,2,128,128]{2,3,0,1:T(8,128)(2,1)} copy(bf16[32,2,128,128]{3,2,1,0:T(8,128)(2,1)} %gather_fusion) | data formatting | bytes 4194304 | tf_op jit(solution)/shard_map/jit(_take)/gather | solution.py:48
  32.9 2.0 %broadcast_select_fusion = bf16[32,2,128,128]{2,3,0,1:T(8,128)(2,1)S(1)} fusion(bf16[32,2,128,128]{2,3,0,1:T(8,128)(2,1)} %copy.49, pred[32]{0:T(512)(128)(4,1)S(1)} %and_bitcast_fusion), kind=kLoop, calls=%fused_computation.17 | loop fusion | flops 1048576 | bytes 4194336 | tf_op jit(solution)/shard_map/jit(_take)/select_n | solution.py:48
  35.2 0.8 fusion.26
  36.0 0.9 subtract_bitcast_fusion
  36.9 0.9 fusion.24
  37.8 14.7 %collective-permute-done = bf16[16,2,128,128]{3,2,0,1:T(8,128)(2,1)} collective-permute-done((bf16[16,2,128,128]{3,2,0,1:T(8,128)(2,1)}, bf16[16,2,128,128]{3,2,0,1:T(8,128)(2,1)}, u32[]{:S(2)}, u32[]{:S(2)}) %collective-permute-start) | collective-permute-done | bytes 1048608 | tf_op jit(solution)/shard_map/ppermute | solution.py:23
  52.5 1.3 fusion.34
  53.8 1.3 fusion.35
  55.1 1.3 fusion.18
  56.5 1.5 %fusion.19 = f32[16,1,128,128]{3,2,0,1:T(8,128)S(1)} fusion(f32[16,128,128]{2,1,0:T(8,128)S(1)} %fusion.35, bf16[16,2,128,128]{3,2,0,1:T(8,128)(2,1)S(1)} %bitcast.293, bf16[16,2,128,128]{3,2,0,1:T(8,128)(2,1)} %collective-permute-done), kind=kOutput, calls=%fused_computation.45 | convolution fusion | flops 67371008 | bytes 3145728 | tf_op jit(solution)/shard_map/nij,njr->nir/dot_general | solution.py:32
  58.5 0.8 collective-permute-start.1
  59.3 0.9 add_bitcast_fusion
  61.7 0.5 fusion.16
  62.2 20.7 %collective-permute-done.1 = bf16[16,2,128,128]{3,2,0,1:T(8,128)(2,1)S(1)} collective-permute-done((bf16[16,2,128,128]{3,2,0,1:T(8,128)(2,1)S(1)}, bf16[16,2,128,128]{3,2,0,1:T(8,128)(2,1)S(1)}, u32[]{:S(2)}, u32[]{:S(2)}) %collective-permute-start.1) | collective-permute-done | bytes 1048608 | tf_op jit(solution)/shard_map/ppermute | solution.py:23
  83.9 0.5 fusion.15
  85.4 2.2 %pad_maximum_fusion = f32[32,2,128,128]{2,3,0,1:T(8,128)} fusion(f32[32,1,128,128]{2,3,0,1:T(8,128)S(1)} %add_bitcast_fusion, f32[32,1,128,128]{2,3,0,1:T(8,128)S(1)} %subtract_bitcast_fusion), kind=kLoop, calls=%fused_computation.2 | loop fusion | flops 1048576 | bytes 8388608 | tf_op jit(solution)/shard_map/stack | solution.py:38
  87.6 5.7 %copy.52 = f32[32,2,128,128]{3,2,1,0:T(8,128)} copy(f32[32,2,128,128]{2,3,0,1:T(8,128)} %pad_maximum_fusion) | data formatting | bytes 8388608 | tf_op jit(solution)/shard_map/stack | solution.py:38
  93.3 4.6 %copy.100 = f32[4,8,256,128]{3,1,2,0:T(8,128)S(1)} copy(f32[4,8,256,128]{3,2,1,0:T(8,128)} %bitcast.265) | data formatting | bytes 8388608
  97.9 0.7 copy.76
  101.1 2.7 %collective-permute-done.2 = bf16[16,2,128,128]{2,3,0,1:T(8,128)(2,1)} collective-permute-done((bf16[16,2,128,128]{2,3,0,1:T(8,128)(2,1)S(1)}, bf16[16,2,128,128]{2,3,0,1:T(8,128)(2,1)}, u32[]{:S(2)}, u32[]{:S(2)}) %collective-permute-start.2) | collective-permute-done | bytes 1048608 | tf_op jit(solution)/shard_map/ppermute | solution.py:23
  103.7 1.5 %fusion.43 = f32[16,128,128]{2,1,0:T(8,128)S(1)} fusion(bf16[16,2,128,128]{2,3,0,1:T(8,128)(2,1)} %collective-permute-done.2, bf16[16,2,128,128]{3,2,0,1:T(8,128)(2,1)S(1)} %bitcast.274), kind=kOutput, calls=%fused_computation.113 | convolution fusion | flops 67108864 | bytes 2097152 | tf_op jit(solution)/shard_map/nij,njr->nir/dot_general | solution.py:32
  105.3 1.5 %fusion.42 = f32[16,128,128]{2,1,0:T(8,128)S(1)} fusion(bf16[16,2,128,128]{2,3,0,1:T(8,128)(2,1)} %collective-permute-done.2, bf16[16,2,128,128]{3,2,0,1:T(8,128)(2,1)S(1)} %bitcast.275), kind=kOutput, calls=%fused_computation.112 | convolution fusion | flops 67108864 | bytes 2097152 | tf_op jit(solution)/shard_map/nij,njr->nir/dot_general | solution.py:35
  106.8 1.5 %fusion.11 = f32[16,1,128,128]{2,3,0,1:T(8,128)S(1)} fusion(f32[16,128,128]{2,1,0:T(8,128)S(1)} %fusion.43, bf16[16,2,128,128]{2,3,0,1:T(8,128)(2,1)} %collective-permute-done.2, bf16[16,2,128,128]{3,2,0,1:T(8,128)(2,1)S(1)} %bitcast.276), kind=kOutput, calls=%fused_computation.29 | convolution fusion | flops 67371008 | bytes 3145728 | tf_op jit(solution)/shard_map/nij,njr->nir/dot_general | solution.py:32
  108.3 1.5 %fusion.10 = f32[16,1,128,128]{2,3,0,1:T(8,128)S(1)} fusion(f32[16,128,128]{2,1,0:T(8,128)S(1)} %fusion.42, bf16[16,2,128,128]{3,2,0,1:T(8,128)(2,1)S(1)} %bitcast.277, bf16[16,2,128,128]{2,3,0,1:T(8,128)(2,1)} %collective-permute-done.2), kind=kOutput, calls=%fused_computation.27 | convolution fusion | flops 67371008 | bytes 3145728 | tf_op jit(solution)/shard_map/nij,njr->nir/dot_general | solution.py:35
  110.2 8.2 %collective-permute-start.3 = (bf16[16,2,128,128]{2,3,0,1:T(8,128)(2,1)S(1)}, bf16[16,2,128,128]{2,3,0,1:T(8,128)(2,1)}, u32[]{:S(2)}, u32[]{:S(2)}) collective-permute-start(bf16[16,2,128,128]{2,3,0,1:T(8,128)(2,1)S(1)} %fusion.4), channel_id=1, source_target_pairs={{0,1},{1,0},{2,3},{3,2},{4,5},{5,4},{6,7},{7,6},{8,9},{9,8},{10,11... | collective-permute-start | bytes 3145736 | tf_op jit(solution)/shard_map/ppermute | solution.py:23
  118.4 5.2 %fusion = f32[16,2,128,128]{3,0,2,1:T(8,128)} fusion(f32[2,128,128,32]{2,1,0,3:T(8,128)S(1)} %bitcast.264, s32[32]{0:T(128)S(1)} %get-tuple-element.15, pred[32]{0:T(512)(128)(4,1)S(1)} %iota_compare_fusion.1), kind=kOutput, calls=%fused_computation.3 | convolution fusion | flops 201327616 | bytes 6291616 | tf_op jit(solution)/shard_map/dot_general | solution.py:54
  123.7 2.9 %copy.54 = f32[16,2,128,128]{2,3,0,1:T(8,128)} copy(f32[16,2,128,128]{3,0,2,1:T(8,128)} %fusion) | data formatting | bytes 4194304 | tf_op jit(solution)/shard_map/dot_general | solution.py:54
  128.6 1.5 %fusion.47 = f32[16,128,128]{2,1,0:T(8,128)S(1)} fusion(bf16[16,2,128,128]{2,3,0,1:T(8,128)(2,1)} %collective-permute-done.3, bf16[16,2,128,128]{3,2,0,1:T(8,128)(2,1)S(1)} %bitcast.266), kind=kOutput, calls=%fused_computation.117 | convolution fusion | flops 67108864 | bytes 2097152 | tf_op jit(solution)/shard_map/nij,njr->nir/dot_general | solution.py:32
  130.1 1.5 %fusion.46 = f32[16,128,128]{2,1,0:T(8,128)S(1)} fusion(bf16[16,2,128,128]{2,3,0,1:T(8,128)(2,1)} %collective-permute-done.3, bf16[16,2,128,128]{3,2,0,1:T(8,128)(2,1)S(1)} %bitcast.267), kind=kOutput, calls=%fused_computation.116 | convolution fusion | flops 67108864 | bytes 2097152 | tf_op jit(solution)/shard_map/nij,njr->nir/dot_general | solution.py:35
  131.6 1.5 %fusion.7 = f32[16,1,128,128]{2,3,0,1:T(8,128)S(1)} fusion(f32[16,128,128]{2,1,0:T(8,128)S(1)} %fusion.47, bf16[16,2,128,128]{2,3,0,1:T(8,128)(2,1)} %collective-permute-done.3, bf16[16,2,128,128]{3,2,0,1:T(8,128)(2,1)S(1)} %bitcast.268), kind=kOutput, calls=%fused_computation.21 | convolution fusion | flops 67371008 | bytes 3145728 | tf_op jit(solution)/shard_map/nij,njr->nir/dot_general | solution.py:32
  133.1 1.7 %fusion.6 = f32[16,1,128,128]{2,3,0,1:T(8,128)S(1)} fusion(f32[16,128,128]{2,1,0:T(8,128)S(1)} %fusion.46, bf16[16,2,128,128]{3,2,0,1:T(8,128)(2,1)S(1)} %bitcast.269, bf16[16,2,128,128]{2,3,0,1:T(8,128)(2,1)} %collective-permute-done.3), kind=kOutput, calls=%fused_computation.19 | convolution fusion | flops 67371008 | bytes 3145728 | tf_op jit(solution)/shard_map/nij,njr->nir/dot_general | solution.py:35
  134.9 0.5 add_convert_fusion
  135.4 1.3 copy.55
  (53 shorter events, 10.5 us)
Async XLA Ops:
  0.0 6.5 %copy-start = (bf16[16,2,128,128]{3,2,1,0:T(8,128)(2,1)S(1)}, bf16[16,2,128,128]{3,2,1,0:T(8,128)(2,1)}, u32[]{:S(2)}) copy-start(bf16[16,2,128,128]{3,2,1,0:T(8,128)(2,1)} %param.6) | copy-start | bytes 3145732
  2.5 50.0 %collective-permute-start = (bf16[16,2,128,128]{3,2,0,1:T(8,128)(2,1)}, bf16[16,2,128,128]{3,2,0,1:T(8,128)(2,1)}, u32[]{:S(2)}, u32[]{:S(2)}) collective-permute-start(bf16[16,2,128,128]{3,2,0,1:T(8,128)(2,1)} %copy.31), channel_id=1, source_target_pairs={{0,8},{1,9},{2,10},{3,11},{4,12},{5,13},{6,14},{7,15},{8,0},{9,1},... | collective-permute-start | bytes 3145736 | tf_op jit(solution)/shard_map/ppermute | solution.py:23
  6.6 16.9 %collective-permute-start.4 = (bf16[8,2,128,128]{3,2,1,0:T(8,128)(2,1)S(1)}, bf16[8,2,128,128]{3,2,1,0:T(8,128)(2,1)S(1)}, u32[]{:S(2)}, u32[]{:S(2)}) collective-permute-start(bf16[8,2,128,128]{3,2,1,0:T(8,128)(2,1)S(1)} %get-tuple-element.13), channel_id=1, source_target_pairs={{0,1},{1,2},{2,3},{3,4},{4,5},{5,6},{6,7},{7,8},{8,9},{9,10},{10,1... | collective-permute-start | bytes 1572872 | tf_op jit(solution)/shard_map/ppermute | solution.py:14
  8.1 15.4 %collective-permute-start.5 = (bf16[8,2,128,128]{3,2,1,0:T(8,128)(2,1)S(1)}, bf16[8,2,128,128]{3,2,1,0:T(8,128)(2,1)S(1)}, u32[]{:S(2)}, u32[]{:S(2)}) collective-permute-start(bf16[8,2,128,128]{3,2,1,0:T(8,128)(2,1)S(1)} %get-tuple-element.14), channel_id=1, source_target_pairs={{1,0},{2,1},{3,2},{4,3},{5,4},{6,5},{7,6},{8,7},{9,8},{10,9},{11,1... | collective-permute-start | bytes 1572872 | tf_op jit(solution)/shard_map/ppermute | solution.py:15
  12.3 2.2 %copy-start.9 = (bf16[4,16,2,128,128]{4,3,2,1,0:T(8,128)(2,1)S(1)}, bf16[4,16,2,128,128]{4,3,2,1,0:T(8,128)(2,1)}, u32[]{:S(2)}) copy-start(bf16[4,16,2,128,128]{4,3,2,1,0:T(8,128)(2,1)} %param.8) | copy-start | bytes 12582916
  20.9 0.7 copy-start.10
  32.9 2.2 %copy-start.6 = (bf16[32,2,128,128]{3,2,1,0:T(8,128)(2,1)S(1)}, bf16[32,2,128,128]{3,2,1,0:T(8,128)(2,1)}, u32[]{:S(2)}) copy-start(bf16[32,2,128,128]{3,2,1,0:T(8,128)(2,1)} %param.9) | copy-start | bytes 6291460
  36.9 15.6 %copy-start.4 = (bf16[1,16,2,128,128]{4,3,1,2,0:T(8,128)(2,1)S(1)}, bf16[1,16,2,128,128]{4,3,1,2,0:T(8,128)(2,1)}, u32[]{:S(2)}) copy-start(bf16[1,16,2,128,128]{4,3,1,2,0:T(8,128)(2,1)} %copy.107) | copy-start | bytes 3145732
  56.5 1.5 %copy-start.7 = (f32[16,1,128,128]{3,2,0,1:T(8,128)S(1)}, f32[16,1,128,128]{3,2,0,1:T(8,128)}, u32[]{:S(2)}) copy-start(f32[16,1,128,128]{3,2,0,1:T(8,128)} %fusion.20) | copy-start | bytes 3145732
  56.5 1.7 %copy-start.8 = (f32[16,1,128,128]{3,2,0,1:T(8,128)S(1)}, f32[16,1,128,128]{3,2,0,1:T(8,128)}, u32[]{:S(2)}) copy-start(f32[16,1,128,128]{3,2,0,1:T(8,128)} %fusion.21) | copy-start | bytes 3145732
  58.5 1.7 %copy-start.3 = (bf16[1,16,2,128,128]{4,3,1,2,0:T(8,128)(2,1)S(1)}, bf16[1,16,2,128,128]{4,3,1,2,0:T(8,128)(2,1)}, u32[]{:S(2)}) copy-start(bf16[1,16,2,128,128]{4,3,1,2,0:T(8,128)(2,1)} %copy.106) | copy-start | bytes 3145732
  58.5 24.4 %collective-permute-start.1 = (bf16[16,2,128,128]{3,2,0,1:T(8,128)(2,1)S(1)}, bf16[16,2,128,128]{3,2,0,1:T(8,128)(2,1)S(1)}, u32[]{:S(2)}, u32[]{:S(2)}) collective-permute-start(bf16[16,2,128,128]{3,2,0,1:T(8,128)(2,1)S(1)} %fusion.2), channel_id=1, source_target_pairs={{0,4},{1,5},{2,6},{3,7},{4,0},{5,1},{6,2},{7,3},{8,12},{9,13},{10,... | collective-permute-start | bytes 3145736 | tf_op jit(solution)/shard_map/ppermute | solution.py:23
  85.3 18.4 %collective-permute-start.2 = (bf16[16,2,128,128]{2,3,0,1:T(8,128)(2,1)S(1)}, bf16[16,2,128,128]{2,3,0,1:T(8,128)(2,1)}, u32[]{:S(2)}, u32[]{:S(2)}) collective-permute-start(bf16[16,2,128,128]{2,3,0,1:T(8,128)(2,1)S(1)} %fusion.3), channel_id=1, source_target_pairs={{0,2},{1,3},{2,0},{3,1},{4,6},{5,7},{6,4},{7,5},{8,10},{9,11},{10,... | collective-permute-start | bytes 3145736 | tf_op jit(solution)/shard_map/ppermute | solution.py:23
  97.9 1.2 copy-start.2
  100.6 3.2 %copy-start.1 = (bf16[1,16,2,128,128]{4,3,1,2,0:T(8,128)(2,1)S(1)}, bf16[1,16,2,128,128]{4,3,1,2,0:T(8,128)(2,1)}, u32[]{:S(2)}) copy-start(bf16[1,16,2,128,128]{4,3,1,2,0:T(8,128)(2,1)} %copy.103) | copy-start | bytes 3145732
  110.2 18.4 %collective-permute-start.3 = (bf16[16,2,128,128]{2,3,0,1:T(8,128)(2,1)S(1)}, bf16[16,2,128,128]{2,3,0,1:T(8,128)(2,1)}, u32[]{:S(2)}, u32[]{:S(2)}) collective-permute-start(bf16[16,2,128,128]{2,3,0,1:T(8,128)(2,1)S(1)} %fusion.4), channel_id=1, source_target_pairs={{0,1},{1,0},{2,3},{3,2},{4,5},{5,4},{6,7},{7,6},{8,9},{9,8},{10,11... | collective-permute-start | bytes 3145736 | tf_op jit(solution)/shard_map/ppermute | solution.py:23
  133.1 1.8 %copy-start.5 = (f32[16,2,128,128]{2,3,0,1:T(8,128)S(1)}, f32[16,2,128,128]{2,3,0,1:T(8,128)}, u32[]{:S(2)}) copy-start(f32[16,2,128,128]{2,3,0,1:T(8,128)} %copy.54) | copy-start | bytes 6291460
where the time goes:
time: 139 us; the launch traced here: 137 us
  waiting for transfers between devices  38 us (27%)
  matrix products  37.6 us (27%)
  local copies, waits for them, and re-layouts  36.9 us (27%)
  starting transfers between devices  15.9 us (11%)
  other arithmetic  7.29 us (5%)
    ppermute x4, waiting for transfers between devices, swapped(): return lax.ppermute(value, axis, pairs)  38 us
    unnamed x33, local copies, waits for them, and re-layouts  15.7 us
    ppermute x4, starting transfers between devices, swapped(): return lax.ppermute(value, axis, pairs)  13.1 us
    dot_general x9, matrix products, complex_apply(): jnp.einsum(form, wi, vi, preferred_element_type=jnp.float32)  8.53 us
    dot_general x9, matrix products, complex_apply(): jnp.einsum(form, wi, vr, preferred_element_type=jnp.float32)  8.5 us
    gather x2, local copies, waits for them, and re-layouts, per_device(): sources = jnp.take(widened, near_pairs[:, 1], axis=0)  7.84 us
    dot_general x9, matrix products, complex_apply(): jnp.einsum(form, wr, vi, preferred_element_type=jnp.float32)  7.68 us
    dot_general x9, matrix products, complex_apply(): jnp.einsum(form, wr, vr, preferred_element_type=jnp.float32)  7.66 us
  transfers between devices with their start and end apart: 6, of which 3 were waited for; matrix products, arithmetic and copies ran while one was open for 39% of the time, Pallas kernels for 0%

commit v1 on v0

v1 whole, which is shorter than its diff:
```python
import functools

import jax
import jax.numpy as jnp
from jax import lax
from jax.experimental import pallas as pl
from jax.experimental.pallas import tpu as pltpu
from jax.sharding import PartitionSpec as P

MESH = pl.DeviceIdType.MESH
WINDOW = 4
LAG = 1
SLOTS_STEP = 4
TARGETS_STEP = 2
ROWS = 32


def stacked(vec):
    vr, vi = vec[0], vec[1]
    return jnp.concatenate(
        [jnp.concatenate([vr, vi], axis=1), jnp.concatenate([-vi, vr], axis=1)], axis=0
    )


def wide(weight):
    return jnp.concatenate([weight[0], weight[1]], axis=1)


def kernel(
    devices,
    pairs_ref,
    count_ref,
    fields_ref,
    own_ref,
    partner_ref,
    blocks_ref,
    out_ref,
    extended,
    own,
    other,
    blocks,
    arrived,
    section,
    products,
    near,
    result,
    send_sem,
    recv_sem,
    halo_send,
    halo_recv,
    field_sem,
    own_sem,
    other_sem,
    block_sem,
    out_sem,
):
    levels, boxes = own_ref.shape[0], own_ref.shape[1]
    slots = blocks_ref.shape[0]
    reach = boxes // 2
    depth = devices.bit_length() - 1
    box, rhs = fields_ref.shape[2], fields_ref.shape[3]
    me = lax.axis_index("leaf")
    has_left, has_right = me > 0, me < devices - 1
    partners = []
    for level in range(levels):
        bit = 2 ** (depth - 1 - level)
        partners.append(jnp.where((me // bit) % 2 == 0, me + bit, me - bit))

    load_fields = pltpu.make_async_copy(
        fields_ref, extended.at[pl.ds(reach, boxes)], field_sem.at[0]
    )
    load_blocks = pltpu.make_async_copy(blocks_ref, blocks, block_sem.at[0])
    load_own = [
        pltpu.make_async_copy(own_ref.at[l], own.at[l], own_sem.at[l]) for l in range(levels)
    ]
    load_other = [
        pltpu.make_async_copy(partner_ref.at[l], other.at[l], other_sem.at[l])
        for l in range(levels)
    ]

    def hop(level, place):
        source = fields_ref.at[place] if level == 0 else section.at[level - 1, place]
        return pltpu.make_async_remote_copy(
            src_ref=source,
            dst_ref=arrived.at[level, place],
            send_sem=send_sem.at[level, place],
            recv_sem=recv_sem.at[level, place],
            device_id={"leaf": partners[level]},
            device_id_type=MESH,
        )

    to_right = pltpu.make_async_remote_copy(
        src_ref=fields_ref.at[pl.ds(boxes - reach, reach)],
        dst_ref=extended.at[pl.ds(0, reach)],
        send_sem=halo_send.at[0],
        recv_sem=halo_recv.at[0],
        device_id={"leaf": jnp.minimum(me + 1, devices - 1)},
        device_id_type=MESH,
    )
    to_left = pltpu.make_async_remote_copy(
        src_ref=fields_ref.at[pl.ds(0, reach)],
        dst_ref=extended.at[pl.ds(reach + boxes, reach)],
        send_sem=halo_send.at[1],
        recv_sem=halo_recv.at[1],
        device_id={"leaf": jnp.maximum(me - 1, 0)},
        device_id_type=MESH,
    )

    def store(place):
        return pltpu.make_async_copy(result.at[place], out_ref.at[place], out_sem.at[place])

    barrier = pltpu.get_barrier_semaphore()
    for level in range(levels):
        pl.semaphore_signal(
            barrier, inc=1, device_id={"leaf": partners[level]}, device_id_type=MESH
        )

    @pl.when(has_left)
    def _():
        pl.semaphore_signal(barrier, inc=1, device_id={"leaf": me - 1}, device_id_type=MESH)

    @pl.when(has_right)
    def _():
        pl.semaphore_signal(barrier, inc=1, device_id={"leaf": me + 1}, device_id_type=MESH)

    load_fields.start()
    for level in range(levels):
        load_own[level].start()
        load_other[level].start()
    load_blocks.start()

    neighbours = jnp.where(has_left, 1, 0) + jnp.where(has_right, 1, 0)
    pl.semaphore_wait(barrier, levels + neighbours)

    for place in range(min(WINDOW, boxes)):
        hop(0, place).start()

    @pl.when(has_right)
    def _():
        to_right.start()

    @pl.when(has_left)
    def _():
        to_left.start()

    load_fields.wait()

    first_product = 2
    first_sum = first_product + slots // SLOTS_STEP
    first_store = first_sum + 1
    steps = max(boxes + (levels - 1) * LAG, first_store + boxes // TARGETS_STEP)

    def step(k, carry):
        @pl.when(k + WINDOW < boxes)
        def _():
            hop(0, k + WINDOW).start()

        for level in range(levels):
            place = k - level * LAG

            @pl.when(place == 0)
            def _():
                load_own[level].wait()
                load_other[level].wait()

            @pl.when((place >= 0) & (place < boxes))
            def _():
                hop(level, place).wait_recv()
                here = extended[reach + place] if level == 0 else section[level - 1, place]
                there = arrived[level, place]
                weights = jnp.concatenate(
                    [wide(own[level, place]), wide(other[level, place])], axis=1
                )
                vectors = jnp.concatenate([stacked(here), stacked(there)], axis=0)
                total = jnp.dot(weights, vectors, preferred_element_type=jnp.float32)
                total = total.astype(jnp.bfloat16)
                section[level, place, 0] = total[:, :rhs]
                section[level, place, 1] = total[:, rhs:]
                if level + 1 < levels:
                    hop(level + 1, place).start()

        @pl.when(k == first_product)
        def _():
            load_blocks.wait()

            @pl.when(has_left)
            def _():
                to_right.wait_recv()

            @pl.when(has_right)
            def _():
                to_left.wait_recv()

        @pl.when((k >= first_product) & (k < first_sum))
        def _():
            for j in range(SLOTS_STEP):
                slot = (k - first_product) * SLOTS_STEP + j
                vec = extended[pairs_ref[slot, 1]]
                products[slot] = jnp.dot(
                    wide(blocks[slot]), stacked(vec), preferred_element_type=jnp.float32
                )

        @pl.when((k >= first_sum) & (k < first_sum + boxes // TARGETS_STEP))
        def _():
            count = count_ref[0]
            first = (k - first_sum) * TARGETS_STEP

            def chunk(c, carry):
                rows = pl.ds(pl.multiple_of(c * ROWS, ROWS), ROWS)
                sums = [jnp.zeros((ROWS, 2 * rhs), jnp.float32) for _ in range(TARGETS_STEP)]
                for slot in range(slots):
                    value = products[slot, rows, :]
                    target = pairs_ref[slot, 0]
                    for j in range(TARGETS_STEP):
                        live = (target == first + j) & (slot < count)
                        sums[j] = sums[j] + jnp.where(live, 1.0, 0.0) * value
                for j in range(TARGETS_STEP):
                    near[first + j, rows, :] = sums[j]
                return carry

            lax.fori_loop(0, box // ROWS, chunk, 0)

        @pl.when(k >= first_store)
        def _():
            for j in range(TARGETS_STEP):
                place = (k - first_store) * TARGETS_STEP + j

                @pl.when(place < boxes)
                def _():
                    for part in range(2):
                        total = section[levels - 1, place, part].astype(jnp.float32)
                        total = total + near[place, :, part * rhs : (part + 1) * rhs]
                        result[place, part] = total.astype(jnp.bfloat16)
                    store(place).start()

        return carry

    lax.fori_loop(0, steps, step, 0)

    def drain(place, carry):
        for level in range(levels):
            hop(level, place).wait_send()
        store(place).wait()
        return carry

    lax.fori_loop(0, boxes, drain, 0)

    @pl.when(has_right)
    def _():
        to_right.wait_send()

    @pl.when(has_left)
    def _():
        to_left.wait_send()


def per_device(fields, own_factor, partner_factor, near_blocks, near_pairs, near_count):
    levels, boxes, _, box, rhs = own_factor.shape[:4] + fields.shape[3:]
    slots = near_blocks.shape[0]
    devices = lax.axis_size("leaf")
    smem = pl.BlockSpec(memory_space=pltpu.SMEM)
    hbm = pl.BlockSpec(memory_space=pl.ANY)
    vector = (2, box, rhs)
    weight = (2, box, box)
    bf16, f32 = jnp.bfloat16, jnp.float32
    dma = pltpu.SemaphoreType.DMA
    products = levels * boxes * 2 + slots
    return pl.pallas_call(
        functools.partial(kernel, devices),
        out_shape=jax.ShapeDtypeStruct(fields.shape, bf16),
        in_specs=[smem, smem, hbm, hbm, hbm, hbm],
        out_specs=hbm,
        scratch_shapes=[
            pltpu.VMEM((2 * boxes,) + vector, bf16),
            pltpu.VMEM((levels, boxes) + weight, bf16),
            pltpu.VMEM((levels, boxes) + weight, bf16),
            pltpu.VMEM((slots,) + weight, bf16),
            pltpu.VMEM((levels, boxes) + vector, bf16),
            pltpu.VMEM((levels, boxes) + vector, bf16),
            pltpu.VMEM((slots, box, 2 * rhs), f32),
            pltpu.VMEM((boxes, box, 2 * rhs), f32),
            pltpu.VMEM((boxes,) + vector, bf16),
            dma((levels, boxes)),
            dma((levels, boxes)),
            dma((2,)),
            dma((2,)),
            dma((1,)),
            dma((levels,)),
            dma((levels,)),
            dma((1,)),
            dma((boxes,)),
        ],
        compiler_params=pltpu.CompilerParams(
            collective_id=0, has_side_effects=True, vmem_limit_bytes=56 * 2**20
        ),
        cost_estimate=pl.CostEstimate(
            flops=8 * products * box * box * rhs,
            bytes_accessed=(products * box * box + 2 * boxes * box * rhs) * 4,
            transcendentals=0,
        ),
    )(near_pairs, near_count, fields, own_factor, partner_factor, near_blocks)


def solution(mesh):
    in_specs = (
        P(("case", "leaf"), None, None, None),
        P(None, ("case", "leaf"), None, None, None),
        P(None, ("case", "leaf"), None, None, None),
        P(("case", "leaf"), None, None, None),
        P("leaf", None),
        P("leaf"),
    )
    out_specs = P(("case", "leaf"), None, None, None)
    return jax.shard_map(
        per_device, mesh=mesh, in_specs=in_specs, out_specs=out_specs, check_vma=False
    )
```

time: 139 us -> 84.7 us (0.61); the launches traced: 137 us -> 83.9 us
  Pallas kernels: 0 us -> 79.6 us
  waiting for transfers between devices: 38 us -> 0 us
  matrix products: 37.6 us -> 0 us
  local copies, waits for them, and re-layouts: 36.9 us -> 3.67 us
  starting transfers between devices: 15.9 us -> 0 us
  other arithmetic: 7.29 us -> 0 us
    pallas_call x0 -> x1, Pallas kernels: none -> 79.6 us  [per_device(): pl.pallas_call(functools.partial(kernel, devices), out_shape=jax.ShapeDty...]
    ppermute x6 -> x0, waiting for transfers between devices: 38 us -> none  [the longest x4 38 us: swapped(): return lax.ppermute(value, axis, pairs)]
    dot_general x37 -> x0, matrix products: 37.6 us -> none  [the longest x9 8.53 us: complex_apply(): jnp.einsum(form, wi, vi, preferred_element_type=jnp.float32)]
    ppermute x6 -> x0, starting transfers between devices: 15.9 us -> none  [the longest x4 13.1 us: swapped(): return lax.ppermute(value, axis, pairs)]
    unnamed x33 -> x2, local copies, waits for them, and re-layouts: 15.7 us -> 3.67 us
    gather x2 -> x0, local copies, waits for them, and re-layouts: 7.84 us -> none  [per_device(): sources = jnp.take(widened, near_pairs[:, 1], axis=0)]
    another operation x1 -> x0, local copies, waits for them, and re-layouts: 5.66 us -> none  [complex_apply(): return jnp.stack([real, imag], axis=1)]
    slice x3 -> x0, local copies, waits for them, and re-layouts: 3.43 us -> none  [the longest x1 2.75 us: per_device(): own_factor[level]]
  transfers between devices with their start and end apart: 6 -> 0, of which waited for: 3 -> 0; matrix products, arithmetic and copies ran while one was open for 39% -> 0% of each run, Pallas kernels for 0% -> 0%
where the time goes in v1:
time: 84.7 us; the launch traced here: 83.9 us
  Pallas kernels  79.6 us (94%)
  local copies, waits for them, and re-layouts  3.67 us (4%)
    pallas_call x1, Pallas kernels, per_device(): pl.pallas_call(functools.partial(kernel, devices), out_shape=jax.ShapeDty...  79.6 us
    unnamed x2, local copies, waits for them, and re-layouts  3.67 us

profile of v1, /device:TPU:0, one launch (start us, length us, event | category | flops | bytes accessed | tf_op | source)
XLA Modules:
  0.0 83.9 jit_solution(14190050795897084886)
XLA Ops:
  0.7 1.4 %copy.7.pairs_ref = s32[32,2]{1,0:T(8,128)} copy(s32[32,2]{0,1:T(2,128)} %param.10) | data formatting | bytes 512 | tf_op args[4]
  2.0 79.6 %shard_map.64 = bf16[16,2,128,128]{3,2,1,0:T(8,128)(2,1)} custom-call(s32[32,2]{1,0:T(8,128)} %copy.7.pairs_ref, s32[1]{0:T(128)S(6)} %copy.9.count_ref, bf16[16,2,128,128]{3,2,1,0:T(8,128)(2,1)} %fields_ref.1, bf16[4,16,2,128,128]{4,3,2,1,0:T(8,128)(2,1)} %own_ref.1, bf16[4,16,2,128,128]{4,3,2,1,0:T(8,128)(2,1)} %partner_ref.1, ...), custom_call_target="tpu_custom_call" | custom-call | flops 2684354560 | bytes 12582912 | tf_op jit(solution)/shard_map/pallas_call | solution.py:268
  81.6 2.3 %copy.10 = bf16[16,2,128,128]{3,2,1,0:T(8,128)(2,1)} copy(bf16[16,2,128,128]{3,2,1,0:T(8,128)(2,1)} %shard_map.64) | data formatting | bytes 2097152

commit v2 on v1

--- a/solution.py
+++ b/solution.py
@@ -9,7 +9,7 @@
 
 MESH = pl.DeviceIdType.MESH
 WINDOW = 4
-LAG = 1
+LAG = 4
 SLOTS_STEP = 4
 TARGETS_STEP = 2
 ROWS = 32
@@ -147,8 +147,9 @@
 
     first_product = 2
     first_sum = first_product + slots // SLOTS_STEP
-    first_store = first_sum + 1
-    steps = max(boxes + (levels - 1) * LAG, first_store + boxes // TARGETS_STEP)
+    store_steps = boxes // TARGETS_STEP
+    first_store = max(first_sum + 1, boxes + (levels - 1) * LAG - store_steps)
+    steps = first_store + store_steps
 
     def step(k, carry):
         @pl.when(k + WINDOW < boxes)
@@ -195,7 +196,7 @@
         def _():
             for j in range(SLOTS_STEP):
                 slot = (k - first_product) * SLOTS_STEP + j
-                vec = extended[pairs_ref[slot, 1]]
+                vec = extended[pairs_ref[1, slot]]
                 products[slot] = jnp.dot(
                     wide(blocks[slot]), stacked(vec), preferred_element_type=jnp.float32
                 )
@@ -210,7 +211,7 @@
                 sums = [jnp.zeros((ROWS, 2 * rhs), jnp.float32) for _ in range(TARGETS_STEP)]
                 for slot in range(slots):
                     value = products[slot, rows, :]
-                    target = pairs_ref[slot, 0]
+                    target = pairs_ref[0, slot]
                     for j in range(TARGETS_STEP):
                         live = (target == first + j) & (slot < count)
                         sums[j] = sums[j] + jnp.where(live, 1.0, 0.0) * value
@@ -298,7 +299,7 @@
             bytes_accessed=(products * box * box + 2 * boxes * box * rhs) * 4,
             transcendentals=0,
         ),
-    )(near_pairs, near_count, fields, own_factor, partner_factor, near_blocks)
+    )(near_pairs.T, near_count, fields, own_factor, partner_factor, near_blocks)
 
 
 def solution(mesh):

time: 84.7 us -> 73.9 us (0.87)
  Pallas kernels: 79.6 us -> 70.7 us
  local copies, waits for them, and re-layouts: 3.67 us -> 2.31 us
    pallas_call x1, Pallas kernels: 79.6 us -> 70.7 us  [per_device(): pl.pallas_call(functools.partial(kernel, devices), out_shape=jax.ShapeDty...]
    unnamed x2 -> x1, local copies, waits for them, and re-layouts: 3.67 us -> 2.31 us
where the time goes in v2:
time: 73.9 us; the launch traced here: 73.7 us
  Pallas kernels  70.7 us (96%)
  local copies, waits for them, and re-layouts  2.31 us (3%)
    pallas_call x1, Pallas kernels, per_device(): pl.pallas_call(functools.partial(kernel, devices), out_shape=jax.ShapeDty...  70.7 us
    unnamed x1, local copies, waits for them, and re-layouts  2.31 us

profile of v2, /device:TPU:0, one launch (start us, length us, event | category | flops | bytes accessed | tf_op | source)
XLA Modules:
  0.0 73.7 jit_solution(17800176957052820538)
XLA Ops:
  0.7 70.7 %shard_map.64 = bf16[16,2,128,128]{3,2,1,0:T(8,128)(2,1)} custom-call(s32[2,32]{1,0:T(2,128)} %bitcast.1, s32[1]{0:T(128)S(6)} %copy.8.count_ref, bf16[16,2,128,128]{3,2,1,0:T(8,128)(2,1)} %fields_ref.1, bf16[4,16,2,128,128]{4,3,2,1,0:T(8,128)(2,1)} %own_ref.1, bf16[4,16,2,128,128]{4,3,2,1,0:T(8,128)(2,1)} %partner_ref.1, bf16[32,2,128,128]{3,2,1,0:T(8,128)(2,1)} %blocks_ref.1), custom_call_target="tpu_custom_call" | custom-call | flops 2684354560 | bytes 12582912 | tf_op jit(solution)/shard_map/pallas_call | solution.py:269
  71.4 2.3 %copy.9 = bf16[16,2,128,128]{3,2,1,0:T(8,128)(2,1)} copy(bf16[16,2,128,128]{3,2,1,0:T(8,128)(2,1)} %shard_map.64) | data formatting | bytes 2097152

commit v3 on v2

--- a/solution.py
+++ b/solution.py
@@ -11,7 +11,7 @@
 WINDOW = 4
 LAG = 4
 SLOTS_STEP = 4
-TARGETS_STEP = 2
+TARGETS_STEP = 4
 ROWS = 32
 
 

time: 73.9 us -> 75.2 us (1.018)
  Pallas kernels: 70.7 us -> 72.1 us
    pallas_call x1, Pallas kernels: 70.7 us -> 72.1 us  [per_device(): pl.pallas_call(functools.partial(kernel, devices), out_shape=jax.ShapeDty...]
where the time goes in v3:
time: 75.2 us; the launch traced here: 75 us
  Pallas kernels  72.1 us (96%)
  local copies, waits for them, and re-layouts  2.31 us (3%)
    pallas_call x1, Pallas kernels, per_device(): pl.pallas_call(functools.partial(kernel, devices), out_shape=jax.ShapeDty...  72.1 us
    unnamed x1, local copies, waits for them, and re-layouts  2.31 us

profile of v3, /device:TPU:0, one launch (start us, length us, event | category | flops | bytes accessed | tf_op | source)
XLA Modules:
  0.0 75.0 jit_solution(14020803605291535312)
XLA Ops:
  0.7 72.1 %shard_map.64 = bf16[16,2,128,128]{3,2,1,0:T(8,128)(2,1)} custom-call(s32[2,32]{1,0:T(2,128)} %bitcast.1, s32[1]{0:T(128)S(6)} %copy.8.count_ref, bf16[16,2,128,128]{3,2,1,0:T(8,128)(2,1)} %fields_ref.1, bf16[4,16,2,128,128]{4,3,2,1,0:T(8,128)(2,1)} %own_ref.1, bf16[4,16,2,128,128]{4,3,2,1,0:T(8,128)(2,1)} %partner_ref.1, bf16[32,2,128,128]{3,2,1,0:T(8,128)(2,1)} %blocks_ref.1), custom_call_target="tpu_custom_call" | custom-call | flops 2684354560 | bytes 12582912 | tf_op jit(solution)/shard_map/pallas_call | solution.py:269
  72.7 2.3 %copy.9 = bf16[16,2,128,128]{3,2,1,0:T(8,128)(2,1)} copy(bf16[16,2,128,128]{3,2,1,0:T(8,128)(2,1)} %shard_map.64) | data formatting | bytes 2097152
